TPU v7x, 512 devices: a whole 4x8x8 slice. The times are simulated.
512 devices in a mesh: gx: 8 (over y), gy: 8 (over z_hi, core), gz: 8 (over x, z_lo).
Axes of the slice: x: 4, y: 8, z: 8 (z_hi: 4, z_lo: 2; z = z_hi * 2 + z_lo), core: 2. Of those that a mesh axis runs over, the one named last changes fastest.
Arguments:
- features: bfloat16 [8, 8, 8, 32, 49, 128], P('gx', 'gy', 'gz'), may hold values from -6 to 6
- border_atoms: int32 [8, 8, 8, 4], P('gx', 'gy', 'gz'), may hold values from 0 to 31, as said below
- inner_source: int32 [8, 8, 8, 128], P('gx', 'gy', 'gz'), may hold values from 0 to 31
- inner_target: int32 [8, 8, 8, 128], P('gx', 'gy', 'gz'), may hold values from 0 to 31
- inner_rotation: int32 [8, 8, 8, 128], P('gx', 'gy', 'gz'), may hold values from 0 to 255
- inner_count: int32 [8, 8, 8], P('gx', 'gy', 'gz'), may hold values from 64 to 128, as said below
- cross_source: int32 [8, 8, 8, 128], P('gx', 'gy', 'gz'), may hold values from 0 to 107, as said below
- cross_target: int32 [8, 8, 8, 128], P('gx', 'gy', 'gz'), may hold values from 0 to 31
- cross_rotation: int32 [8, 8, 8, 2, 128], P('gx', 'gy', 'gz'), may hold values from 0 to 255
- cross_count: int32 [8, 8, 8], P('gx', 'gy', 'gz'), may hold values from 64 to 128, as said below
- rotations: bfloat16 [49, 49, 256], replicated, as said below
- order_zero: bfloat16 [896, 896], P(('gy', 'gz')), may hold values from -0.1875 to 0.1875
- order_one: bfloat16 [2, 768, 768], P(None, ('gy', 'gz')), may hold values from -0.15625 to 0.15625
- order_two: bfloat16 [2, 640, 640], P(None, ('gy', 'gz')), may hold values from -0.15625 to 0.15625
Outputs:
- updated: bfloat16 [8, 8, 8, 32, 49, 128], P('gx', 'gy', 'gz')
Inputs may be any that keep to these rules, and one draw needn't show every extreme that they name: `border_atoms`: 4 different atoms of the cell. `inner_count`: edges at positions below the count are live; some cell has all 128 live. `cross_count`: edges at positions below the count are live; some cell has all 128 live. `cross_source`: a row s * 4 + t of around with s never 13, the cell itself. An entry rotations[i, j, r] is zero unless i and j have the same degree.
All inputs are finite; a program needn't handle non-finite values.
Results may differ from a plain program's by a relative error of at most 0.006.
Values may be sent and summed in bfloat16 or wider, within the bound.
No kernel may reach another device: no remote copies, remote signals or barrier semaphores. Data moves between devices by JAX's collectives and lax.ppermute only.
A program may use at most 128 MiB of HBM per device.

v0:
```python
import math
import jax
import jax.numpy as jnp
import numpy as np
from jax import lax
from jax.sharding import PartitionSpec as P

LMAX = 6


def extended(block, sides, width):
    for axis, dim in sides:
        count = lax.axis_size(axis)
        forward = [(i, i + 1) for i in range(count - 1)]
        forward.append((count - 1, 0))
        backward = [(target, source) for source, target in forward]
        low = lax.ppermute(
            lax.slice_in_dim(block, block.shape[dim] - width, None, axis=dim), axis, forward
        )
        high = lax.ppermute(lax.slice_in_dim(block, 0, width, axis=dim), axis, backward)
        block = jnp.concatenate([low, block, high], axis=dim)
    return block


def kept_rows(top_degree):
    listing = [d * d + d for d in range(top_degree + 1)]
    for shift in (1, -1, 2, -2):
        listing = listing + [d * d + d + shift for d in range(abs(shift), top_degree + 1)]
    return np.array(listing, dtype=np.int32)


def conv_messages(sources, chosen, full_zero, full_one, full_two):
    row_total = sources.shape[0]
    channels = sources.shape[2]
    size_zero = LMAX + 1
    size_one = LMAX
    size_two = LMAX - 1
    turned = jnp.einsum("nrj,njc->nrc", chosen, sources, preferred_element_type=jnp.float32).astype(
        jnp.bfloat16
    )
    zero_part = turned[:, :size_zero].reshape(row_total, size_zero * channels)
    plus_one = turned[:, size_zero : size_zero + size_one].reshape(row_total, size_one * channels)
    minus_one = turned[:, size_zero + size_one : size_zero + 2 * size_one].reshape(
        row_total, size_one * channels
    )
    two_start = size_zero + 2 * size_one
    plus_two = turned[:, two_start : two_start + size_two].reshape(row_total, size_two * channels)
    minus_two = turned[:, two_start + size_two : two_start + 2 * size_two].reshape(
        row_total, size_two * channels
    )
    out_zero = jnp.dot(zero_part, full_zero, preferred_element_type=jnp.float32)
    out_plus1 = jnp.dot(plus_one, full_one[0], preferred_element_type=jnp.float32) - jnp.dot(
        minus_one, full_one[1], preferred_element_type=jnp.float32
    )
    out_minus1 = jnp.dot(minus_one, full_one[0], preferred_element_type=jnp.float32) + jnp.dot(
        plus_one, full_one[1], preferred_element_type=jnp.float32
    )
    out_plus2 = jnp.dot(plus_two, full_two[0], preferred_element_type=jnp.float32) - jnp.dot(
        minus_two, full_two[1], preferred_element_type=jnp.float32
    )
    out_minus2 = jnp.dot(minus_two, full_two[0], preferred_element_type=jnp.float32) + jnp.dot(
        plus_two, full_two[1], preferred_element_type=jnp.float32
    )
    pieces = [out_zero, out_plus1, out_minus1, out_plus2, out_minus2]
    mixed = jnp.concatenate(
        [piece.reshape(row_total, -1, channels) for piece in pieces], axis=1
    ).astype(jnp.bfloat16)
    return jnp.einsum("nrj,nrc->njc", chosen, mixed, preferred_element_type=jnp.float32)


def collect(total, source_table, sources, targets, picked, live, trimmed, weights):
    edge_total = sources.shape[0]
    block_size = math.gcd(128, edge_total)

    def advance(running, position):
        first_edge = position * block_size
        live_mask = (first_edge + jnp.arange(block_size, dtype=jnp.int32) < live).astype(
            jnp.float32
        )
        chosen = jnp.transpose(trimmed[:, :, picked], (2, 0, 1))
        result = conv_messages(source_table[sources], chosen, weights[0], weights[1], weights[2])
        result = result * live_mask[:, None, None]
        running = running.at[targets].add(result.reshape(block_size, -1))
        return (running, None)

    total, _ = lax.scan(advance, total, jnp.arange(edge_total // block_size, dtype=jnp.int32))
    return total


def fold_sides(padded, axis_dim):
    lower = lax.slice_in_dim(padded, 0, 1, axis=axis_dim)
    middle = lax.slice_in_dim(padded, 2, 3, axis=axis_dim)
    upper = lax.slice_in_dim(padded, 4, 5, axis=axis_dim)
    return lower + middle + upper


def fold_x(partial_value):
    padded = extended(partial_value.astype(jnp.bfloat16), (("gx", 0),), 1).astype(
        partial_value.dtype
    )
    return fold_sides(padded, 0)


def fold_y(partial_value):
    padded = extended(partial_value.astype(jnp.bfloat16), (("gy", 1),), 1).astype(
        partial_value.dtype
    )
    return fold_sides(padded, 1)


def fold_z(partial_value):
    padded = extended(partial_value.astype(jnp.bfloat16), (("gz", 2),), 1).astype(
        partial_value.dtype
    )
    return fold_sides(padded, 2)


def shards(
    features,
    border_atoms,
    inner_source,
    inner_target,
    inner_rotation,
    inner_count,
    cross_source,
    cross_target,
    cross_rotation,
    cross_count,
    rotations,
    order_zero,
    order_one,
    order_two,
):
    full_zero, full_one, full_two = (
        lax.all_gather(order_zero, ("gy", "gz"), axis=0, tiled=True),
        lax.all_gather(order_one, ("gy", "gz"), axis=1, tiled=True),
        lax.all_gather(order_two, ("gy", "gz"), axis=1, tiled=True),
    )
    weights = (full_zero, full_one, full_two)
    local_atoms = features[0, 0, 0]
    atom_total = local_atoms.shape[0]
    harmonics = local_atoms.shape[1]
    channels = local_atoms.shape[2]
    border_rows = border_atoms[0, 0, 0]
    border_total = border_rows.shape[0]
    border = local_atoms[border_rows].reshape(1, 1, 1, border_total, harmonics, channels)
    beside_all = extended(border, (("gx", 0), ("gy", 1), ("gz", 2)), 1)
    beside_all = beside_all.reshape(27 * border_total, harmonics, channels)
    trimmed = rotations[jnp.asarray(kept_rows(LMAX)), :, :]
    gathered = jnp.zeros((atom_total, harmonics * channels), jnp.float32)
    gathered = collect(
        gathered,
        local_atoms,
        inner_source[0, 0, 0],
        inner_target[0, 0, 0],
        inner_rotation[0, 0, 0],
        inner_count[0, 0, 0],
        trimmed,
        weights,
    )
    gathered = collect(
        gathered,
        beside_all,
        cross_source[0, 0, 0],
        cross_target[0, 0, 0],
        cross_rotation[0, 0, 0, 0],
        cross_count[0, 0, 0],
        trimmed,
        weights,
    )
    returned = jnp.zeros((27 * border_total, harmonics * channels), jnp.float32)
    returned = collect(
        returned,
        local_atoms,
        cross_target[0, 0, 0],
        cross_source[0, 0, 0],
        cross_rotation[0, 0, 0, 1],
        cross_count[0, 0, 0],
        trimmed,
        weights,
    )
    returned = returned.reshape(3, 3, 3, border_total, harmonics * channels)
    returned = fold_z(fold_y(fold_x(returned)))
    gathered = gathered.at[border_rows].add(returned.reshape(border_total, -1))
    updated = local_atoms.astype(jnp.float32) + 0.25 * gathered.reshape(
        atom_total, harmonics, channels
    )
    return updated.astype(jnp.bfloat16).reshape(features.shape)


def solution(mesh):
    in_specs = (
        P("gx", "gy", "gz", None, None, None),
        P("gx", "gy", "gz", None),
        P("gx", "gy", "gz", None),
        P("gx", "gy", "gz", None),
        P("gx", "gy", "gz", None),
        P("gx", "gy", "gz"),
        P("gx", "gy", "gz", None),
        P("gx", "gy", "gz", None),
        P("gx", "gy", "gz", None, None),
        P("gx", "gy", "gz"),
        P(),
        P(("gy", "gz"), None),
        P(None, ("gy", "gz"), None),
        P(None, ("gy", "gz"), None),
    )
    out_specs = P("gx", "gy", "gz", None, None, None)
    return jax.shard_map(shards, mesh=mesh, in_specs=in_specs, out_specs=out_specs, check_vma=False)
```

profile of v0, /device:TPU:129, one launch (start us, length us, event | category | flops | bytes accessed | tf_op | source)
XLA Modules:
  0.0 741.7 jit_solution(9208425399380260902)
XLA Ops:
  11.1 5.1 collective-permute-start.1
  21.5 4.1 copy.200
  30.1 2.5 convolution_convert_fusion
  43.0 2.9 collective-permute-start.3
  45.9 6.9 collective-permute-start.2
  57.1 6.1 collective-permute-start.5
  63.2 2.4 collective-permute-start.4
  79.2 7.3 collective-permute-done.4
  95.7 105.9 %all-gather.9.cloned.1.call-done = bf16[64,14,896]{2,1,0:T(8,128)(2,1)} async-done(((bf16[1,14,896]{2,1,0:T(8,128)(2,1)}), bf16[64,14,896]{2,1,0:T(8,128)(2,1)}) %all-gather.9.cloned.1.call-update) | async-done | bytes 1605648 | tf_op jit(solution)/shard_map/all_gather | solution.py:135
  201.6 3.7 reshape.612
  205.3 2.9 copy.203
  212.2 184.6 %all-gather.7.cloned.1.call-done = bf16[2,640,640]{2,0,1:T(2,128)(2,1)} async-done(((bf16[2,10,640]{2,0,1:T(2,128)(2,1)}), bf16[2,640,640]{2,0,1:T(2,128)(2,1)}) %all-gather.7.cloned.1.call-update) | async-done | bytes 1638416 | tf_op jit(solution)/shard_map/all_gather | solution.py:137
  396.8 4.8 fusion.53
  411.9 177.2 %all-gather.5.cloned.1.call-done = bf16[2,768,768]{2,0,1:T(2,128)(2,1)} async-done(((bf16[2,12,768]{2,0,1:T(2,128)(2,1)}), bf16[2,768,768]{2,0,1:T(2,128)(2,1)}) %all-gather.5.cloned.1.call-update) | async-done | bytes 2359312 | tf_op jit(solution)/shard_map/all_gather | solution.py:136
  589.1 6.4 fusion.52
  606.6 4.6 convolution_multiply_fusion
  611.2 4.7 copy.260
  615.9 4.9 copy.261
  620.8 7.5 %scatter_custom_fusion.2 = f32[108,6272]{1,0:T(8,128)} fusion(s32[128]{0:T(128)S(1)} %fusion.50, f32[128,6272]{1,0:T(8,128)} %copy.261, f32[]{:T(128)} %constant.37.clone.1), kind=kCustom, calls=%fused_computation.19 | custom fusion | flops 802816 | bytes 2710016 | tf_op jit(solution)/shard_map/while/body/eval_jaxpr/scatter-add | solution.py:83
  632.3 3.5 convert_element_type.88
  650.7 4.6 collective-permute-start.7
  661.8 4.4 convolution_multiply_fusion.1
  668.0 11.9 %collective-permute-start.8 = (bf16[1,1,3,4,6272]{4,3,2,1,0:T(4,128)(2,1)S(1)}, bf16[1,1,3,4,6272]{4,3,2,1,0:T(4,128)(2,1)S(1)}, u32[]{:S(2)}, u32[]{:S(2)}) collective-permute-start(bf16[1,1,3,4,6272]{4,3,2,1,0:T(4,128)(2,1)S(1)} %get-tuple-element.98), channel_id=1, source_target_pairs={{0,8},{8,16},{16,24},{24,32},{32,40},{40,48},{48,56},{56,0},{1,9},... | collective-permute-start | bytes 451592 | tf_op jit(solution)/shard_map/ppermute | solution.py:17
  682.4 7.7 %collective-permute-done.9 = bf16[1,1,3,4,6272]{4,3,2,1,0:T(4,128)(2,1)S(1)} collective-permute-done((bf16[1,1,3,4,6272]{4,3,2,1,0:T(4,128)(2,1)S(1)}, bf16[1,1,3,4,6272]{4,3,2,1,0:T(4,128)(2,1)S(1)}, u32[]{:S(2)}, u32[]{:S(2)}) %collective-permute-start.9) | collective-permute-done | bytes 150560 | tf_op jit(solution)/shard_map/ppermute | solution.py:20
  692.4 5.5 collective-permute-start.11
  697.8 3.2 convolution_multiply_fusion.2
  701.0 4.5 copy.222
  705.5 4.9 copy.223
  710.3 4.5 copy.242
  714.8 4.9 copy.243
  719.7 6.0 scatter_custom_fusion
  725.7 6.3 scatter_fusion
  (223 shorter events, 110.1 us)
Async XLA Ops:
  6.5 14.4 %copy-start = (bf16[49,49,256]{2,1,0:T(8,128)(2,1)S(1)}, bf16[49,49,256]{2,1,0:T(8,128)(2,1)}, u32[]{:S(2)}) copy-start(bf16[49,49,256]{2,1,0:T(8,128)(2,1)} %param.25) | copy-start | bytes 3687940
  6.5 195.0 %all-gather.9.cloned.1.call-start = ((), (), s32[]{:S(2)}) async-start(), calls=%async_computation.2 | async-start | bytes 1863680 | tf_op jit(solution)/shard_map/all_gather | solution.py:135
  7.3 389.5 %all-gather.7.cloned.1.call-start = ((), (), s32[]{:S(2)}) async-start(), calls=%async_computation.1 | async-start | bytes 1664000 | tf_op jit(solution)/shard_map/all_gather | solution.py:137
  8.0 581.1 %all-gather.5.cloned.1.call-start = ((), (), s32[]{:S(2)}) async-start(), calls=%async_computation | async-start | bytes 2396160 | tf_op jit(solution)/shard_map/all_gather | solution.py:136
  11.1 31.9 %collective-permute-start.1 = (bf16[1,1,1,4,49,128]{5,4,3,2,1,0:T(8,128)(2,1)S(1)}, bf16[1,1,1,4,49,128]{5,4,3,2,1,0:T(8,128)(2,1)S(1)}, u32[]{:S(2)}, u32[]{:S(2)}) collective-permute-start(bf16[1,1,1,4,49,128]{5,4,3,2,1,0:T(8,128)(2,1)S(1)} %bitcast.192), channel_id=1, source_target_pairs={{64,0},{128,64},{192,128},{256,192},{320,256},{384,320},{448,384},... | collective-permute-start | bytes 150536 | tf_op jit(solution)/shard_map/ppermute | solution.py:20
  16.2 26.8 %collective-permute-start = (bf16[1,1,1,4,49,128]{5,4,3,2,1,0:T(8,128)(2,1)S(1)}, bf16[1,1,1,4,49,128]{5,4,3,2,1,0:T(8,128)(2,1)S(1)}, u32[]{:S(2)}, u32[]{:S(2)}) collective-permute-start(bf16[1,1,1,4,49,128]{5,4,3,2,1,0:T(8,128)(2,1)S(1)} %bitcast.193), channel_id=1, source_target_pairs={{0,64},{64,128},{128,192},{192,256},{256,320},{320,384},{384,448},... | collective-permute-start | bytes 150536 | tf_op jit(solution)/shard_map/ppermute | solution.py:17
  41.0 24.7 %copy-start.9 = (bf16[128,29,128]{2,1,0:T(8,128)(2,1)}, bf16[128,29,128]{2,1,0:T(8,128)(2,1)S(1)}, u32[]{:S(2)}) copy-start(bf16[128,29,128]{2,1,0:T(8,128)(2,1)S(1)} %convolution_convert_fusion.2) | copy-start | bytes 2850820
  41.0 11.8 %copy-start.35 = (s32[1,1,1,128]{3,2,1,0:T(1,128)S(1)}, s32[1,1,1,128]{3,2,1,0:T(1,128)}, u32[]{:S(2)}) copy-start(s32[1,1,1,128]{3,2,1,0:T(1,128)} %param.21) | copy-start | bytes 1540
  43.0 22.7 %copy-start.33 = (bf16[1,1,1,4,49,128]{5,4,3,2,1,0:T(8,128)(2,1)}, bf16[1,1,1,4,49,128]{5,4,3,2,1,0:T(8,128)(2,1)S(1)}, u32[]{:S(2)}) copy-start(bf16[1,1,1,4,49,128]{5,4,3,2,1,0:T(8,128)(2,1)S(1)} %collective-permute-done.1) | copy-start | bytes 150532
  43.0 22.7 %copy-start.34 = (bf16[1,1,1,4,49,128]{5,4,3,2,1,0:T(8,128)(2,1)}, bf16[1,1,1,4,49,128]{5,4,3,2,1,0:T(8,128)(2,1)S(1)}, u32[]{:S(2)}) copy-start(bf16[1,1,1,4,49,128]{5,4,3,2,1,0:T(8,128)(2,1)S(1)} %collective-permute-done) | copy-start | bytes 150532
  43.0 12.1 %collective-permute-start.3 = (bf16[3,1,1,4,49,128]{5,4,3,2,1,0:T(8,128)(2,1)S(1)}, bf16[3,1,1,4,49,128]{5,4,3,2,1,0:T(8,128)(2,1)S(1)}, u32[]{:S(2)}, u32[]{:S(2)}) collective-permute-start(bf16[3,1,1,4,49,128]{5,4,3,2,1,0:T(8,128)(2,1)S(1)} %pad_maximum_fusion.4), channel_id=1, source_target_pairs={{8,0},{16,8},{24,16},{32,24},{40,32},{48,40},{56,48},{0,56},{9,1},... | collective-permute-start | bytes 451592 | tf_op jit(solution)/shard_map/ppermute | solution.py:20
  45.9 10.3 %collective-permute-start.2 = (bf16[3,1,1,4,49,128]{5,4,3,2,1,0:T(8,128)(2,1)S(1)}, bf16[3,1,1,4,49,128]{5,4,3,2,1,0:T(8,128)(2,1)S(1)}, u32[]{:S(2)}, u32[]{:S(2)}) collective-permute-start(bf16[3,1,1,4,49,128]{5,4,3,2,1,0:T(8,128)(2,1)S(1)} %pad_maximum_fusion.4), channel_id=1, source_target_pairs={{0,8},{8,16},{16,24},{24,32},{32,40},{40,48},{48,56},{56,0},{1,9},... | collective-permute-start | bytes 451592 | tf_op jit(solution)/shard_map/ppermute | solution.py:17
  55.1 12.0 %copy-start.27 = (bf16[3,1,1,4,49,128]{5,4,3,2,1,0:T(8,128)(2,1)}, bf16[3,1,1,4,49,128]{5,4,3,2,1,0:T(8,128)(2,1)S(1)}, u32[]{:S(2)}) copy-start(bf16[3,1,1,4,49,128]{5,4,3,2,1,0:T(8,128)(2,1)S(1)} %collective-permute-done.3) | copy-start | bytes 451588
  56.2 9.4 %copy-start.28 = (bf16[3,1,1,4,49,128]{5,4,3,2,1,0:T(8,128)(2,1)}, bf16[3,1,1,4,49,128]{5,4,3,2,1,0:T(8,128)(2,1)S(1)}, u32[]{:S(2)}) copy-start(bf16[3,1,1,4,49,128]{5,4,3,2,1,0:T(8,128)(2,1)S(1)} %collective-permute-done.2) | copy-start | bytes 451588
  57.1 22.1 %collective-permute-start.5 = (bf16[3,3,1,4,49,128]{5,4,3,2,1,0:T(8,128)(2,1)}, bf16[3,3,1,4,49,128]{5,4,3,2,1,0:T(8,128)(2,1)}, u32[]{:S(2)}, u32[]{:S(2)}) collective-permute-start(bf16[3,3,1,4,49,128]{5,4,3,2,1,0:T(8,128)(2,1)} %pad_maximum_fusion.1), channel_id=1, source_target_pairs={{1,0},{2,1},{3,2},{4,3},{5,4},{6,5},{7,6},{0,7},{9,8},{10,9},{11,1... | collective-permute-start | bytes 1354760 | tf_op jit(solution)/shard_map/ppermute | solution.py:20
  63.2 23.3 %collective-permute-start.4 = (bf16[3,3,1,4,49,128]{5,4,3,2,1,0:T(8,128)(2,1)}, bf16[3,3,1,4,49,128]{5,4,3,2,1,0:T(8,128)(2,1)}, u32[]{:S(2)}, u32[]{:S(2)}) collective-permute-start(bf16[3,3,1,4,49,128]{5,4,3,2,1,0:T(8,128)(2,1)} %pad_maximum_fusion.1), channel_id=1, source_target_pairs={{0,1},{1,2},{2,3},{3,4},{4,5},{5,6},{6,7},{7,0},{8,9},{9,10},{10,1... | collective-permute-start | bytes 1354760 | tf_op jit(solution)/shard_map/ppermute | solution.py:17
  65.8 10.3 %slice-start = ((bf16[128,29,128]{2,1,0:T(8,128)(2,1)}), bf16[128,7,128]{2,1,0:T(8,128)(2,1)S(1)}, s32[]{:S(2)}) async-start(bf16[128,29,128]{2,1,0:T(8,128)(2,1)} %copy-done.9), calls=%async_computation.3 | async-start | bytes 524288 | tf_op jit(solution)/shard_map/while/body/eval_jaxpr/slice | solution.py:41
  67.1 9.9 %copy-start.22 = (bf16[128,5,128]{2,1,0:T(8,128)(2,1)S(1)}, bf16[128,5,128]{2,1,0:T(8,128)(2,1)}, u32[]{:S(2)}) copy-start(bf16[128,5,128]{2,1,0:T(8,128)(2,1)} %get-tuple-element.94) | copy-start | bytes 491524
  69.5 20.6 %copy-start.5 = (bf16[128,29,49]{2,1,0:T(8,128)(2,1)}, bf16[128,29,49]{2,1,0:T(8,128)(2,1)S(1)}, u32[]{:S(2)}) copy-start(bf16[128,29,49]{2,1,0:T(8,128)(2,1)S(1)} %gather_fusion.3) | copy-start | bytes 1091332
  649.1 9.9 %copy-start.32 = (bf16[128,5,128]{2,0,1:T(8,128)(2,1)S(1)}, bf16[128,5,128]{2,0,1:T(8,128)(2,1)}, u32[]{:S(2)}) copy-start(bf16[128,5,128]{2,0,1:T(8,128)(2,1)} %copy.239) | copy-start | bytes 491524
  650.4 10.7 %copy-start.30 = (bf16[128,5,128]{2,0,1:T(8,128)(2,1)S(1)}, bf16[128,5,128]{2,0,1:T(8,128)(2,1)}, u32[]{:S(2)}) copy-start(bf16[128,5,128]{2,0,1:T(8,128)(2,1)} %copy.240) | copy-start | bytes 491524
  650.4 11.4 %copy-start.6 = (bf16[128,29,49]{2,1,0:T(8,128)(2,1)S(1)}, bf16[128,29,49]{2,1,0:T(8,128)(2,1)}, u32[]{:S(2)}) copy-start(bf16[128,29,49]{2,1,0:T(8,128)(2,1)} %copy-done.5) | copy-start | bytes 1091332
  650.7 15.5 %collective-permute-start.7 = (bf16[1,3,3,4,6272]{4,3,2,1,0:T(4,128)(2,1)S(1)}, bf16[1,3,3,4,6272]{4,3,2,1,0:T(4,128)(2,1)S(1)}, u32[]{:S(2)}, u32[]{:S(2)}) collective-permute-start(bf16[1,3,3,4,6272]{4,3,2,1,0:T(4,128)(2,1)S(1)} %slice.185), channel_id=1, source_target_pairs={{64,0},{128,64},{192,128},{256,192},{320,256},{384,320},{448,384},... | collective-permute-start | bytes 1354760 | tf_op jit(solution)/shard_map/ppermute | solution.py:20
  655.3 11.6 %collective-permute-start.6 = (bf16[1,3,3,4,6272]{4,3,2,1,0:T(4,128)(2,1)}, bf16[1,3,3,4,6272]{4,3,2,1,0:T(4,128)(2,1)S(1)}, u32[]{:S(2)}, u32[]{:S(2)}) collective-permute-start(bf16[1,3,3,4,6272]{4,3,2,1,0:T(4,128)(2,1)} %slice.183), channel_id=1, source_target_pairs={{0,64},{64,128},{128,192},{192,256},{256,320},{320,384},{384,448},... | collective-permute-start | bytes 1354760 | tf_op jit(solution)/shard_map/ppermute | solution.py:17
  666.2 15.7 %copy-start.14 = (bf16[128,29,128]{2,0,1:T(8,128)(2,1)S(1)}, bf16[128,29,128]{2,0,1:T(8,128)(2,1)}, u32[]{:S(2)}) copy-start(bf16[128,29,128]{2,0,1:T(8,128)(2,1)} %constant_dynamic-update-slice_fusion.2) | copy-start | bytes 2850820
  666.2 15.7 %copy-start.31 = (bf16[128,5,128]{2,0,1:T(8,128)(2,1)S(1)}, bf16[128,5,128]{2,0,1:T(8,128)(2,1)}, u32[]{:S(2)}) copy-start(bf16[128,5,128]{2,0,1:T(8,128)(2,1)} %copy.219) | copy-start | bytes 491524
  666.2 15.7 %copy-start.29 = (bf16[128,5,128]{2,0,1:T(8,128)(2,1)S(1)}, bf16[128,5,128]{2,0,1:T(8,128)(2,1)}, u32[]{:S(2)}) copy-start(bf16[128,5,128]{2,0,1:T(8,128)(2,1)} %copy.220) | copy-start | bytes 491524
  667.8 30.0 %copy-start.4 = (bf16[128,29,49]{2,1,0:T(8,128)(2,1)S(1)}, bf16[128,29,49]{2,1,0:T(8,128)(2,1)}, u32[]{:S(2)}) copy-start(bf16[128,29,49]{2,1,0:T(8,128)(2,1)} %copy-done.3) | copy-start | bytes 1091332
  668.0 14.4 %collective-permute-start.8 = (bf16[1,1,3,4,6272]{4,3,2,1,0:T(4,128)(2,1)S(1)}, bf16[1,1,3,4,6272]{4,3,2,1,0:T(4,128)(2,1)S(1)}, u32[]{:S(2)}, u32[]{:S(2)}) collective-permute-start(bf16[1,1,3,4,6272]{4,3,2,1,0:T(4,128)(2,1)S(1)} %get-tuple-element.98), channel_id=1, source_target_pairs={{0,8},{8,16},{16,24},{24,32},{32,40},{40,48},{48,56},{56,0},{1,9},... | collective-permute-start | bytes 451592 | tf_op jit(solution)/shard_map/ppermute | solution.py:17
  679.9 10.2 %collective-permute-start.9 = (bf16[1,1,3,4,6272]{4,3,2,1,0:T(4,128)(2,1)S(1)}, bf16[1,1,3,4,6272]{4,3,2,1,0:T(4,128)(2,1)S(1)}, u32[]{:S(2)}, u32[]{:S(2)}) collective-permute-start(bf16[1,1,3,4,6272]{4,3,2,1,0:T(4,128)(2,1)S(1)} %get-tuple-element.110), channel_id=1, source_target_pairs={{8,0},{16,8},{24,16},{32,24},{40,32},{48,40},{56,48},{0,56},{9,1},... | collective-permute-start | bytes 451592 | tf_op jit(solution)/shard_map/ppermute | solution.py:20
  690.4 41.5 %collective-permute-start.10 = (bf16[1,1,1,4,6272]{4,3,2,1,0:T(4,128)(2,1)S(1)}, bf16[1,1,1,4,6272]{4,3,2,1,0:T(4,128)(2,1)S(1)}, u32[]{:S(2)}, u32[]{:S(2)}) collective-permute-start(bf16[1,1,1,4,6272]{4,3,2,1,0:T(4,128)(2,1)S(1)} %get-tuple-element.111), channel_id=1, source_target_pairs={{0,1},{1,2},{2,3},{3,4},{4,5},{5,6},{6,7},{7,0},{8,9},{9,10},{10,1... | collective-permute-start | bytes 150536 | tf_op jit(solution)/shard_map/ppermute | solution.py:17
  692.4 39.6 %collective-permute-start.11 = (bf16[1,1,1,4,6272]{4,3,2,1,0:T(4,128)(2,1)S(1)}, bf16[1,1,1,4,6272]{4,3,2,1,0:T(4,128)(2,1)S(1)}, u32[]{:S(2)}, u32[]{:S(2)}) collective-permute-start(bf16[1,1,1,4,6272]{4,3,2,1,0:T(4,128)(2,1)S(1)} %get-tuple-element.112), channel_id=1, source_target_pairs={{1,0},{2,1},{3,2},{4,3},{5,4},{6,5},{7,6},{0,7},{9,8},{10,9},{11,1... | collective-permute-start | bytes 150536 | tf_op jit(solution)/shard_map/ppermute | solution.py:20
  (21 other events, 65.0 us)
Sparse Core Ops, SparseCore 0:
  9.5 192.0 all-gather.8
  203.7 193.0 all-gather.6
  398.9 190.2 all-gather.4
where the time goes:
time: 748 us; the launch traced here: 742 us
  waiting for transfers between devices  489 us (65%)
  local copies, waits for them, and re-layouts  116 us (16%)
  starting transfers between devices  53.6 us (7%)
  matrix products  36.7 us (5%)
  other arithmetic  31.6 us (4%)
  between operations  15.5 us (2%)
    all_gather x1, waiting for transfers between devices, shards(): lax.all_gather(order_two, ('gy', 'gz'), axis=1, tiled=True)  185 us
    all_gather x1, waiting for transfers between devices, shards(): lax.all_gather(order_one, ('gy', 'gz'), axis=1, tiled=True)  177 us
    all_gather x1, waiting for transfers between devices, shards(): lax.all_gather(order_zero, ('gy', 'gz'), axis=0, tiled=True)  106 us
    ppermute x6, starting transfers between devices, extended(): lax.ppermute(lax.slice_in_dim(block, block.shape[dim] - width, None, axis...  27.5 us
    ppermute x6, starting transfers between devices, extended(): lax.ppermute(lax.slice_in_dim(block, 0, width, axis=dim), axis, backward)  26 us
    scatter-add x3, other arithmetic, advance(): running = running.at[targets].add(result.reshape(block_size, -1))  19.8 us
  transfers between devices with their start and end apart: 15, of which 9 were waited for; matrix products, arithmetic and copies ran while one was open for 16% of the time, Pallas kernels for 0%

commit v1 on v0

--- a/solution.py
+++ b/solution.py
@@ -6,6 +6,11 @@
 from jax.sharding import PartitionSpec as P
 
 LMAX = 6
+
+
+def exchange_gather(shard, name, dim):
+    sent = jnp.stack([shard] * lax.axis_size(name))
+    return jnp.concatenate(lax.all_to_all(sent, name, 0, 0), axis=dim)
 
 
 def extended(block, sides, width):
@@ -134,7 +139,7 @@
     full_zero, full_one, full_two = (
         lax.all_gather(order_zero, ("gy", "gz"), axis=0, tiled=True),
         lax.all_gather(order_one, ("gy", "gz"), axis=1, tiled=True),
-        lax.all_gather(order_two, ("gy", "gz"), axis=1, tiled=True),
+        exchange_gather(order_two, ("gy", "gz"), 1),
     )
     weights = (full_zero, full_one, full_two)
     local_atoms = features[0, 0, 0]

time: 748 us -> 574 us (0.77)
  waiting for transfers between devices: 489 us -> 281 us
  local copies, waits for them, and re-layouts: 116 us -> 133 us
  starting transfers between devices: 53.6 us -> 63.1 us
    all_gather x1 -> x0, waiting for transfers between devices: 185 us -> none  [shards(): lax.all_gather(order_two, ('gy', 'gz'), axis=1, tiled=True)]
    all_gather x1, waiting for transfers between devices: 106 us -> 91.6 us  [shards(): lax.all_gather(order_zero, ('gy', 'gz'), axis=0, tiled=True)]
    all_gather x1, waiting for transfers between devices: 177 us -> 163 us  [shards(): lax.all_gather(order_one, ('gy', 'gz'), axis=1, tiled=True)]
    all_to_all x0 -> x1, starting transfers between devices: none -> 12.8 us  [exchange_gather(): return jnp.concatenate(lax.all_to_all(sent, name, 0, 0), axis=dim)]
    ppermute x6, waiting for transfers between devices: 9.93 us -> 18.5 us  [extended(): lax.ppermute(lax.slice_in_dim(block, 0, width, axis=dim), axis, backward)]
    unnamed x85 -> x101, local copies, waits for them, and re-layouts: 14.5 us -> 17.6 us
  transfers between devices with their start and end apart: 15 -> 15, of which waited for: 9 -> 7; matrix products, arithmetic and copies ran while one was open for 16% -> 23% of each run, Pallas kernels for 0% -> 0%
where the time goes in v1:
time: 574 us; the launch traced here: 563 us
  waiting for transfers between devices  281 us (49%)
  local copies, waits for them, and re-layouts  133 us (23%)
  starting transfers between devices  63.1 us (11%)
  matrix products  39.7 us (7%)
  other arithmetic  30.7 us (5%)
  between operations  15.9 us (3%)
    all_gather x1, waiting for transfers between devices, shards(): lax.all_gather(order_one, ('gy', 'gz'), axis=1, tiled=True)  163 us
    all_gather x1, waiting for transfers between devices, shards(): lax.all_gather(order_zero, ('gy', 'gz'), axis=0, tiled=True)  91.6 us
    ppermute x6, starting transfers between devices, extended(): lax.ppermute(lax.slice_in_dim(block, 0, width, axis=dim), axis, backward)  25.2 us
    ppermute x6, starting transfers between devices, extended(): lax.ppermute(lax.slice_in_dim(block, block.shape[dim] - width, None, axis...  25.1 us
    scatter-add x3, other arithmetic, advance(): running = running.at[targets].add(result.reshape(block_size, -1))  19.6 us
    ppermute x6, waiting for transfers between devices, extended(): lax.ppermute(lax.slice_in_dim(block, 0, width, axis=dim), axis, backward)  18.5 us
    unnamed x101, local copies, waits for them, and re-layouts  17.6 us
    all_to_all x1, starting transfers between devices, exchange_gather(): return jnp.concatenate(lax.all_to_all(sent, name, 0, 0), axis=dim)  12.8 us
  transfers between devices with their start and end apart: 15, of which 7 were waited for; matrix products, arithmetic and copies ran while one was open for 23% of the time, Pallas kernels for 0%

profile of v1, /device:TPU:129, one launch (start us, length us, event | category | flops | bytes accessed | tf_op | source)
XLA Modules:
  0.0 563.4 jit_solution(1091475274353131737)
XLA Ops:
  10.9 5.1 collective-permute-start.1
  18.0 2.8 stack.2
  20.7 12.8 %all-to-all-start = ((bf16[64,2,10,640]{3,1,2,0:T(2,128)(2,1)}), bf16[64,2,10,640]{3,1,2,0:T(2,128)(2,1)S(1)}, u32[]{:S(2)}, u32[]{:S(2)}) async-start(bf16[64,2,10,640]{3,1,2,0:T(2,128)(2,1)} %stack.2), calls=%async_computation | async-start | bytes 3276800 | tf_op jit(solution)/shard_map/all_to_all | solution.py:13
  35.9 5.1 copy.199
  61.0 5.4 collective-permute-start.2
  66.5 10.8 %collective-permute-done.3 = bf16[3,1,1,4,49,128]{5,4,3,2,1,0:T(8,128)(2,1)S(1)} collective-permute-done((bf16[3,1,1,4,49,128]{5,4,3,2,1,0:T(8,128)(2,1)S(1)}, bf16[3,1,1,4,49,128]{5,4,3,2,1,0:T(8,128)(2,1)S(1)}, u32[]{:S(2)}, u32[]{:S(2)}) %collective-permute-start.3) | collective-permute-done | bytes 150560 | tf_op jit(solution)/shard_map/ppermute | solution.py:25
  79.8 5.8 %collective-permute-start.5 = (bf16[3,3,1,4,49,128]{5,4,3,2,1,0:T(8,128)(2,1)}, bf16[3,3,1,4,49,128]{5,4,3,2,1,0:T(8,128)(2,1)}, u32[]{:S(2)}, u32[]{:S(2)}) collective-permute-start(bf16[3,3,1,4,49,128]{5,4,3,2,1,0:T(8,128)(2,1)} %pad_maximum_fusion.1), channel_id=1, source_target_pairs={{1,0},{2,1},{3,2},{4,3},{5,4},{6,5},{7,6},{0,7},{9,8},{10,9},{11,1... | collective-permute-start | bytes 1354760 | tf_op jit(solution)/shard_map/ppermute | solution.py:25
  89.0 3.3 gather_fusion.3
  102.9 5.4 collective-permute-done.4
  119.0 91.6 %all-gather.6.cloned.1.call-done = bf16[64,14,896]{2,1,0:T(8,128)(2,1)} async-done(((bf16[1,14,896]{2,1,0:T(8,128)(2,1)}), bf16[64,14,896]{2,1,0:T(8,128)(2,1)}) %all-gather.6.cloned.1.call-update) | async-done | bytes 1605648 | tf_op jit(solution)/shard_map/all_gather | solution.py:140
  210.6 3.8 reshape.623
  214.4 2.9 copy.202
  222.3 9.3 %slice_reduce_fusion = (bf16[64,10,640]{2,1,0:T(8,128)(2,1)}, bf16[64,10,640]{2,1,0:T(8,128)(2,1)}) fusion(bf16[2,64,10,640]{3,0,2,1:T(2,128)(2,1)S(1)} %bitcast.157), kind=kLoop, calls=%fused_computation.15 | loop fusion | bytes 3276800 | tf_op jit(solution)/shard_map/while/body/eval_jaxpr/slice | solution.py:64
  243.9 163.5 %all-gather.4.cloned.1.call-done = bf16[2,768,768]{2,0,1:T(2,128)(2,1)} async-done(((bf16[2,12,768]{2,0,1:T(2,128)(2,1)}), bf16[2,768,768]{2,0,1:T(2,128)(2,1)}) %all-gather.4.cloned.1.call-update) | async-done | bytes 2359312 | tf_op jit(solution)/shard_map/all_gather | solution.py:141
  407.4 6.4 %fusion.52 = (bf16[1,768,768]{2,0,1:T(2,128)(2,1)S(1)}, bf16[1,768,768]{2,0,1:T(2,128)(2,1)S(1)}) fusion(bf16[2,768,768]{2,0,1:T(2,128)(2,1)} %all-gather.4.cloned.1.call-done), kind=kLoop, calls=%fused_computation.133 | loop fusion | bytes 4718592 | tf_op jit(solution)/shard_map/while/body/eval_jaxpr/slice | solution.py:58
  429.8 4.3 convolution_multiply_fusion
  434.0 4.5 copy.257
  438.5 5.3 copy.258
  443.8 7.5 %scatter_custom_fusion.2 = f32[108,6272]{1,0:T(8,128)} fusion(s32[128]{0:T(128)S(1)} %fusion.50, f32[128,6272]{1,0:T(8,128)} %copy.258, f32[]{:T(128)} %constant.37.clone.1), kind=kCustom, calls=%fused_computation.21 | custom fusion | flops 802816 | bytes 2710016 | tf_op jit(solution)/shard_map/while/body/eval_jaxpr/scatter-add | solution.py:88
  454.5 3.5 convert_element_type.88
  477.4 4.4 collective-permute-start.7
  488.4 4.4 convolution_multiply_fusion.1
  494.4 11.9 %collective-permute-start.8 = (bf16[1,1,3,4,6272]{4,3,2,1,0:T(4,128)(2,1)S(1)}, bf16[1,1,3,4,6272]{4,3,2,1,0:T(4,128)(2,1)S(1)}, u32[]{:S(2)}, u32[]{:S(2)}) collective-permute-start(bf16[1,1,3,4,6272]{4,3,2,1,0:T(4,128)(2,1)S(1)} %get-tuple-element.98), channel_id=1, source_target_pairs={{0,8},{8,16},{16,24},{24,32},{32,40},{40,48},{48,56},{56,0},{1,9},... | collective-permute-start | bytes 451592 | tf_op jit(solution)/shard_map/ppermute | solution.py:22
  508.9 7.7 %collective-permute-done.9 = bf16[1,1,3,4,6272]{4,3,2,1,0:T(4,128)(2,1)S(1)} collective-permute-done((bf16[1,1,3,4,6272]{4,3,2,1,0:T(4,128)(2,1)S(1)}, bf16[1,1,3,4,6272]{4,3,2,1,0:T(4,128)(2,1)S(1)}, u32[]{:S(2)}, u32[]{:S(2)}) %collective-permute-start.9) | collective-permute-done | bytes 150560 | tf_op jit(solution)/shard_map/ppermute | solution.py:25
  518.9 5.5 collective-permute-start.11
  524.4 3.1 convolution_multiply_fusion.2
  527.5 3.7 copy.219
  531.1 3.1 copy.220
  534.2 3.7 copy.239
  537.9 3.1 copy.240
  541.0 6.0 %scatter_custom_fusion = f32[32,6272]{1,0:T(8,128)S(1)} fusion(s32[128]{0:T(128)S(1)} %fusion.44, f32[128,6272]{1,0:T(8,128)} %copy.220, f32[]{:T(128)} %constant.37.clone.1), kind=kCustom, calls=%fused_computation.68 | custom fusion | flops 802816 | bytes 803328 | tf_op jit(solution)/shard_map/while/body/eval_jaxpr/scatter-add | solution.py:88
  547.0 6.1 %scatter_fusion = f32[32,6272]{1,0:T(8,128)S(1)} fusion(f32[32,6272]{1,0:T(8,128)S(1)} %scatter_custom_fusion, s32[128]{0:T(128)S(1)} %fusion.47, f32[128,6272]{1,0:T(8,128)} %copy.240), kind=kCustom, calls=%fused_computation.9 | custom fusion | flops 802816 | bytes 9634304 | tf_op jit(solution)/shard_map/while/body/eval_jaxpr/scatter-add | solution.py:88
  (241 shorter events, 125.9 us)
Async XLA Ops:
  6.5 27.9 %copy-start = (bf16[49,49,256]{2,1,0:T(8,128)(2,1)S(1)}, bf16[49,49,256]{2,1,0:T(8,128)(2,1)}, u32[]{:S(2)}) copy-start(bf16[49,49,256]{2,1,0:T(8,128)(2,1)} %param.25) | copy-start | bytes 3687940
  6.5 204.1 %all-gather.6.cloned.1.call-start = ((), (), s32[]{:S(2)}) async-start(), calls=%async_computation.2 | async-start | bytes 1863680 | tf_op jit(solution)/shard_map/all_gather | solution.py:140
  10.9 46.9 %collective-permute-start.1 = (bf16[1,1,1,4,49,128]{5,4,3,2,1,0:T(8,128)(2,1)}, bf16[1,1,1,4,49,128]{5,4,3,2,1,0:T(8,128)(2,1)}, u32[]{:S(2)}, u32[]{:S(2)}) collective-permute-start(bf16[1,1,1,4,49,128]{5,4,3,2,1,0:T(8,128)(2,1)} %bitcast.31), channel_id=1, source_target_pairs={{64,0},{128,64},{192,128},{256,192},{320,256},{384,320},{448,384},... | collective-permute-start | bytes 150536 | tf_op jit(solution)/shard_map/ppermute | solution.py:25
  16.0 41.8 %collective-permute-start = (bf16[1,1,1,4,49,128]{5,4,3,2,1,0:T(8,128)(2,1)}, bf16[1,1,1,4,49,128]{5,4,3,2,1,0:T(8,128)(2,1)}, u32[]{:S(2)}, u32[]{:S(2)}) collective-permute-start(bf16[1,1,1,4,49,128]{5,4,3,2,1,0:T(8,128)(2,1)} %bitcast.31), channel_id=1, source_target_pairs={{0,64},{64,128},{128,192},{192,256},{256,320},{320,384},{384,448},... | collective-permute-start | bytes 150536 | tf_op jit(solution)/shard_map/ppermute | solution.py:22
  20.7 13.6 %copy-start.41 = (s32[1,1,1,128]{3,2,1,0:T(1,128)S(1)}, s32[1,1,1,128]{3,2,1,0:T(1,128)}, u32[]{:S(2)}) copy-start(s32[1,1,1,128]{3,2,1,0:T(1,128)} %param.22) | copy-start | bytes 1540
  20.7 13.6 %copy-start.42 = (s32[1,1,1,128]{3,2,1,0:T(1,128)S(1)}, s32[1,1,1,128]{3,2,1,0:T(1,128)}, u32[]{:S(2)}) copy-start(s32[1,1,1,128]{3,2,1,0:T(1,128)} %param.19) | copy-start | bytes 1540
  20.7 13.7 %copy-start.39 = (s32[1,1,1,2,128]{4,3,2,1,0:T(2,128)S(1)}, s32[1,1,1,2,128]{4,3,2,1,0:T(2,128)}, u32[]{:S(2)}) copy-start(s32[1,1,1,2,128]{4,3,2,1,0:T(2,128)} %param.23) | copy-start | bytes 3076
  20.7 13.7 %copy-start.40 = (s32[29]{0:T(128)S(1)}, s32[29]{0:T(128)}, u32[]{:S(2)}) copy-start(s32[29]{0:T(128)} %constant.80) | copy-start | bytes 352
  20.7 201.5 %all-to-all-start = ((bf16[64,2,10,640]{3,1,2,0:T(2,128)(2,1)}), bf16[64,2,10,640]{3,1,2,0:T(2,128)(2,1)S(1)}, u32[]{:S(2)}, u32[]{:S(2)}) async-start(bf16[64,2,10,640]{3,1,2,0:T(2,128)(2,1)} %stack.2), calls=%async_computation | async-start | bytes 3276800 | tf_op jit(solution)/shard_map/all_to_all | solution.py:13
  33.6 373.8 %all-gather.4.cloned.1.call-start = ((), (), s32[]{:S(2)}) async-start(), calls=%async_computation.1 | async-start | bytes 2396160 | tf_op jit(solution)/shard_map/all_gather | solution.py:141
  56.7 30.9 %copy-start.10 = (bf16[128,29,128]{2,1,0:T(8,128)(2,1)}, bf16[128,29,128]{2,1,0:T(8,128)(2,1)S(1)}, u32[]{:S(2)}) copy-start(bf16[128,29,128]{2,1,0:T(8,128)(2,1)S(1)} %convolution_convert_fusion.2) | copy-start | bytes 2850820
  57.8 34.4 %slice-start = ((bf16[128,29,128]{2,1,0:T(8,128)(2,1)}), bf16[128,7,128]{2,1,0:T(8,128)(2,1)S(1)}, s32[]{:S(2)}) async-start(bf16[128,29,128]{2,1,0:T(8,128)(2,1)} %copy-done.9), calls=%async_computation.3 | async-start | bytes 524288 | tf_op jit(solution)/shard_map/while/body/eval_jaxpr/slice | solution.py:46
  58.8 18.6 %collective-permute-start.3 = (bf16[3,1,1,4,49,128]{5,4,3,2,1,0:T(8,128)(2,1)S(1)}, bf16[3,1,1,4,49,128]{5,4,3,2,1,0:T(8,128)(2,1)S(1)}, u32[]{:S(2)}, u32[]{:S(2)}) collective-permute-start(bf16[3,1,1,4,49,128]{5,4,3,2,1,0:T(8,128)(2,1)S(1)} %pad_maximum_fusion.4), channel_id=1, source_target_pairs={{8,0},{16,8},{24,16},{32,24},{40,32},{48,40},{56,48},{0,56},{9,1},... | collective-permute-start | bytes 451592 | tf_op jit(solution)/shard_map/ppermute | solution.py:25
  61.0 16.3 %collective-permute-start.2 = (bf16[3,1,1,4,49,128]{5,4,3,2,1,0:T(8,128)(2,1)S(1)}, bf16[3,1,1,4,49,128]{5,4,3,2,1,0:T(8,128)(2,1)S(1)}, u32[]{:S(2)}, u32[]{:S(2)}) collective-permute-start(bf16[3,1,1,4,49,128]{5,4,3,2,1,0:T(8,128)(2,1)S(1)} %pad_maximum_fusion.4), channel_id=1, source_target_pairs={{0,8},{8,16},{16,24},{24,32},{32,40},{40,48},{48,56},{56,0},{1,9},... | collective-permute-start | bytes 451592 | tf_op jit(solution)/shard_map/ppermute | solution.py:22
  79.8 15.2 %copy-start.25 = (bf16[128,6,128]{2,1,0:T(8,128)(2,1)S(1)}, bf16[128,6,128]{2,1,0:T(8,128)(2,1)}, u32[]{:S(2)}) copy-start(bf16[128,6,128]{2,1,0:T(8,128)(2,1)} %get-tuple-element.88) | copy-start | bytes 589828
  79.8 23.1 %collective-permute-start.5 = (bf16[3,3,1,4,49,128]{5,4,3,2,1,0:T(8,128)(2,1)}, bf16[3,3,1,4,49,128]{5,4,3,2,1,0:T(8,128)(2,1)}, u32[]{:S(2)}, u32[]{:S(2)}) collective-permute-start(bf16[3,3,1,4,49,128]{5,4,3,2,1,0:T(8,128)(2,1)} %pad_maximum_fusion.1), channel_id=1, source_target_pairs={{1,0},{2,1},{3,2},{4,3},{5,4},{6,5},{7,6},{0,7},{9,8},{10,9},{11,1... | collective-permute-start | bytes 1354760 | tf_op jit(solution)/shard_map/ppermute | solution.py:25
  85.6 22.6 %collective-permute-start.4 = (bf16[3,3,1,4,49,128]{5,4,3,2,1,0:T(8,128)(2,1)}, bf16[3,3,1,4,49,128]{5,4,3,2,1,0:T(8,128)(2,1)}, u32[]{:S(2)}, u32[]{:S(2)}) collective-permute-start(bf16[3,3,1,4,49,128]{5,4,3,2,1,0:T(8,128)(2,1)} %pad_maximum_fusion.1), channel_id=1, source_target_pairs={{0,1},{1,2},{2,3},{3,4},{4,5},{5,6},{6,7},{7,0},{8,9},{9,10},{10,1... | collective-permute-start | bytes 1354760 | tf_op jit(solution)/shard_map/ppermute | solution.py:22
  96.7 11.6 %copy-start.33 = (bf16[3,1,1,4,49,128]{5,4,3,2,1,0:T(8,128)(2,1)S(1)}, bf16[3,1,1,4,49,128]{5,4,3,2,1,0:T(8,128)(2,1)}, u32[]{:S(2)}) copy-start(bf16[3,1,1,4,49,128]{5,4,3,2,1,0:T(8,128)(2,1)} %copy-done.32) | copy-start | bytes 451588
  417.6 12.2 %copy-start.7 = (bf16[128,29,49]{2,1,0:T(8,128)(2,1)S(1)}, bf16[128,29,49]{2,1,0:T(8,128)(2,1)}, u32[]{:S(2)}) copy-start(bf16[128,29,49]{2,1,0:T(8,128)(2,1)} %copy-done.6) | copy-start | bytes 1091332
  474.3 11.7 %copy-start.38 = (bf16[128,5,128]{2,0,1:T(8,128)(2,1)S(1)}, bf16[128,5,128]{2,0,1:T(8,128)(2,1)}, u32[]{:S(2)}) copy-start(bf16[128,5,128]{2,0,1:T(8,128)(2,1)} %copy.236) | copy-start | bytes 491524
  474.3 12.4 %copy-start.17 = (bf16[128,29,128]{2,0,1:T(8,128)(2,1)S(1)}, bf16[128,29,128]{2,0,1:T(8,128)(2,1)}, u32[]{:S(2)}) copy-start(bf16[128,29,128]{2,0,1:T(8,128)(2,1)} %fusion.2) | copy-start | bytes 2850820
  476.3 11.4 %copy-start.36 = (bf16[128,5,128]{2,0,1:T(8,128)(2,1)S(1)}, bf16[128,5,128]{2,0,1:T(8,128)(2,1)}, u32[]{:S(2)}) copy-start(bf16[128,5,128]{2,0,1:T(8,128)(2,1)} %copy.237) | copy-start | bytes 491524
  476.3 12.2 %copy-start.5 = (bf16[128,29,49]{2,1,0:T(8,128)(2,1)S(1)}, bf16[128,29,49]{2,1,0:T(8,128)(2,1)}, u32[]{:S(2)}) copy-start(bf16[128,29,49]{2,1,0:T(8,128)(2,1)} %gather_fusion.3) | copy-start | bytes 1091332
  477.4 15.4 %collective-permute-start.7 = (bf16[1,3,3,4,6272]{4,3,2,1,0:T(4,128)(2,1)}, bf16[1,3,3,4,6272]{4,3,2,1,0:T(4,128)(2,1)S(1)}, u32[]{:S(2)}, u32[]{:S(2)}) collective-permute-start(bf16[1,3,3,4,6272]{4,3,2,1,0:T(4,128)(2,1)} %slice.187), channel_id=1, source_target_pairs={{64,0},{128,64},{192,128},{256,192},{320,256},{384,320},{448,384},... | collective-permute-start | bytes 1354760 | tf_op jit(solution)/shard_map/ppermute | solution.py:25
  481.8 11.6 %collective-permute-start.6 = (bf16[1,3,3,4,6272]{4,3,2,1,0:T(4,128)(2,1)}, bf16[1,3,3,4,6272]{4,3,2,1,0:T(4,128)(2,1)S(1)}, u32[]{:S(2)}, u32[]{:S(2)}) collective-permute-start(bf16[1,3,3,4,6272]{4,3,2,1,0:T(4,128)(2,1)} %slice.185), channel_id=1, source_target_pairs={{0,64},{64,128},{128,192},{192,256},{256,320},{320,384},{384,448},... | collective-permute-start | bytes 1354760 | tf_op jit(solution)/shard_map/ppermute | solution.py:22
  492.8 15.7 %copy-start.37 = (bf16[128,5,128]{2,0,1:T(8,128)(2,1)S(1)}, bf16[128,5,128]{2,0,1:T(8,128)(2,1)}, u32[]{:S(2)}) copy-start(bf16[128,5,128]{2,0,1:T(8,128)(2,1)} %copy.216) | copy-start | bytes 491524
  492.8 15.7 %copy-start.35 = (bf16[128,5,128]{2,0,1:T(8,128)(2,1)S(1)}, bf16[128,5,128]{2,0,1:T(8,128)(2,1)}, u32[]{:S(2)}) copy-start(bf16[128,5,128]{2,0,1:T(8,128)(2,1)} %copy.217) | copy-start | bytes 491524
  494.3 30.0 %copy-start.4 = (bf16[128,29,49]{2,1,0:T(8,128)(2,1)S(1)}, bf16[128,29,49]{2,1,0:T(8,128)(2,1)}, u32[]{:S(2)}) copy-start(bf16[128,29,49]{2,1,0:T(8,128)(2,1)} %copy-done.3) | copy-start | bytes 1091332
  494.4 14.5 %collective-permute-start.8 = (bf16[1,1,3,4,6272]{4,3,2,1,0:T(4,128)(2,1)S(1)}, bf16[1,1,3,4,6272]{4,3,2,1,0:T(4,128)(2,1)S(1)}, u32[]{:S(2)}, u32[]{:S(2)}) collective-permute-start(bf16[1,1,3,4,6272]{4,3,2,1,0:T(4,128)(2,1)S(1)} %get-tuple-element.98), channel_id=1, source_target_pairs={{0,8},{8,16},{16,24},{24,32},{32,40},{40,48},{48,56},{56,0},{1,9},... | collective-permute-start | bytes 451592 | tf_op jit(solution)/shard_map/ppermute | solution.py:22
  506.4 10.2 %collective-permute-start.9 = (bf16[1,1,3,4,6272]{4,3,2,1,0:T(4,128)(2,1)S(1)}, bf16[1,1,3,4,6272]{4,3,2,1,0:T(4,128)(2,1)S(1)}, u32[]{:S(2)}, u32[]{:S(2)}) collective-permute-start(bf16[1,1,3,4,6272]{4,3,2,1,0:T(4,128)(2,1)S(1)} %get-tuple-element.110), channel_id=1, source_target_pairs={{8,0},{16,8},{24,16},{32,24},{40,32},{48,40},{56,48},{0,56},{9,1},... | collective-permute-start | bytes 451592 | tf_op jit(solution)/shard_map/ppermute | solution.py:25
  516.9 36.1 %collective-permute-start.10 = (bf16[1,1,1,4,6272]{4,3,2,1,0:T(4,128)(2,1)S(1)}, bf16[1,1,1,4,6272]{4,3,2,1,0:T(4,128)(2,1)S(1)}, u32[]{:S(2)}, u32[]{:S(2)}) collective-permute-start(bf16[1,1,1,4,6272]{4,3,2,1,0:T(4,128)(2,1)S(1)} %get-tuple-element.111), channel_id=1, source_target_pairs={{0,1},{1,2},{2,3},{3,4},{4,5},{5,6},{6,7},{7,0},{8,9},{9,10},{10,1... | collective-permute-start | bytes 150536 | tf_op jit(solution)/shard_map/ppermute | solution.py:22
  518.9 34.2 %collective-permute-start.11 = (bf16[1,1,1,4,6272]{4,3,2,1,0:T(4,128)(2,1)S(1)}, bf16[1,1,1,4,6272]{4,3,2,1,0:T(4,128)(2,1)}, u32[]{:S(2)}, u32[]{:S(2)}) collective-permute-start(bf16[1,1,1,4,6272]{4,3,2,1,0:T(4,128)(2,1)S(1)} %get-tuple-element.112), channel_id=1, source_target_pairs={{1,0},{2,1},{3,2},{4,3},{5,4},{6,5},{7,6},{0,7},{9,8},{10,9},{11,1... | collective-permute-start | bytes 150536 | tf_op jit(solution)/shard_map/ppermute | solution.py:25
  (30 other events, 115.1 us)
Sparse Core Ops, SparseCore 0:
  9.5 201.0 all-gather.5
  212.7 194.6 all-gather.3
